TPU v7x, 256 devices: a whole 4x4x8 slice. The times are simulated.
256 devices in a mesh: row: 4 (over z_hi), col: 8 (over z_lo, y), depth: 8 (over x, core).
Axes of the slice: x: 4, y: 4, z: 8 (z_hi: 4, z_lo: 2; z = z_hi * 2 + z_lo), core: 2. Of those that a mesh axis runs over, the one named last changes fastest.
Arguments:
- tokens: bfloat16 [6144, 8192], P('col', 'depth'), may hold values from -6 to 6
- weight: bfloat16 [4096, 3, 8192], P(('row', 'col'), None, 'depth'), may hold values from -0.0625 to 0.0625
- taps: float32 [7, 256], P(None, 'row'), may hold values from -3 to 3
- upstream: bfloat16 [6144, 4096], P(('col', 'depth'), 'row'), may hold values from -6 to 6
Outputs:
- output: bfloat16 [6144, 4096], P(('col', 'depth'), 'row')
- grad_tokens: bfloat16 [6144, 8192], P('col', 'depth')
- grad_weight: float32 [4096, 3, 8192], P(('row', 'col'), None, 'depth')
- grad_taps: float32 [7, 256], P(None, 'row')
All inputs are finite; a program needn't handle non-finite values.
Results may differ from a plain program's by a relative error of at most 0.034.
Values may be sent and summed in bfloat16 or wider, within the bound.
A program may use at most 128 MiB of HBM per device.

v0:
```python
import jax
import jax.numpy as jnp
from jax import lax
from jax.sharding import PartitionSpec as P

GROUP = 16
KT = 7


def passed_along(value, axis, steps):
    count = lax.axis_size(axis)
    leading, last = (max(0, -steps), min(count, count - steps))
    return lax.ppermute(value, axis, [(source, source + steps) for source in range(leading, last)])


def on_device(tokens, weight, taps, upstream):
    local_tok = upstream.shape[0]
    channels = upstream.shape[1]
    margin = KT - 1
    panel_full = lax.all_gather(weight, "col", axis=0, tiled=True)
    summed_proj = lax.psum_scatter(
        jnp.einsum("td,csd->tsc", tokens, panel_full, preferred_element_type=jnp.float32).astype(
            jnp.bfloat16
        ),
        "depth",
        scatter_dimension=0,
        tiled=True,
    )
    rounded = lax.optimization_barrier(summed_proj).astype(jnp.float32)
    query_part = rounded[:, 0, :]
    key_part = rounded[:, 1, :]
    value_part = rounded[:, 2, :]
    mixed = key_part * value_part
    spread = jnp.repeat(taps, GROUP, axis=1)
    earlier = passed_along(mixed[local_tok - margin :], ("col", "depth"), 1)
    padded = jnp.concatenate([earlier, mixed], 0)
    filtered = jnp.zeros((local_tok, channels), jnp.float32)
    for offset in range(KT):
        first_row = margin - offset
        filtered = filtered + spread[offset] * padded[first_row : first_row + local_tok]
    output = (query_part * filtered).astype(jnp.bfloat16)
    upstream_f = upstream.astype(jnp.float32)
    grad_query = upstream_f * filtered
    grad_filtered = upstream_f * query_part
    later = passed_along(grad_filtered[:margin], ("col", "depth"), -1)
    padded_grad = jnp.concatenate([grad_filtered, later], 0)
    grad_mixed = jnp.zeros((local_tok, channels), jnp.float32)
    for offset in range(KT):
        grad_mixed = grad_mixed + spread[offset] * padded_grad[offset : offset + local_tok]
    grad_key = grad_mixed * value_part
    grad_value = grad_mixed * key_part
    grad_proj = jnp.stack([grad_query, grad_key, grad_value], axis=1).astype(jnp.bfloat16)
    tap_rows = []
    for offset in range(KT):
        first_row = margin - offset
        summed = jnp.sum(grad_filtered * padded[first_row : first_row + local_tok], axis=0)
        tap_rows.append(summed.reshape(-1, GROUP).sum(axis=1))
    grad_taps = lax.psum(jnp.stack(tap_rows, 0), ("col", "depth"))
    grad_group = lax.all_gather(grad_proj, "depth", axis=0, tiled=True)
    grad_weight = lax.psum_scatter(
        jnp.einsum("tsc,td->csd", grad_group, tokens, preferred_element_type=jnp.float32).astype(
            jnp.bfloat16
        ),
        "col",
        scatter_dimension=0,
        tiled=True,
    ).astype(jnp.float32)
    partial_in = jnp.einsum(
        "tsc,csd->td", grad_group, panel_full, preferred_element_type=jnp.float32
    )
    grad_tokens = lax.psum(partial_in.astype(jnp.bfloat16), "row")
    return (output, grad_tokens, grad_weight, grad_taps)


def solution(mesh):
    in_specs = (
        P("col", "depth"),
        P(("row", "col"), None, "depth"),
        P(None, "row"),
        P(("col", "depth"), "row"),
    )
    out_specs = (
        P(("col", "depth"), "row"),
        P("col", "depth"),
        P(("row", "col"), None, "depth"),
        P(None, "row"),
    )
    return jax.shard_map(
        on_device, mesh=mesh, in_specs=in_specs, out_specs=out_specs, check_vma=False
    )
```

profile of v0, /device:TPU:1, one launch (start us, length us, event | category | flops | bytes accessed | tf_op | source)
XLA Modules:
  0.0 413.7 jit_solution(10683279714632097685)
XLA Ops:
  7.2 0.7 all-gather.3.cloned.1.call-update
  8.0 80.6 %all-gather.3.cloned.1.call-done = bf16[1024,3,1024]{2,0,1:T(8,128)(2,1)} async-done(((bf16[128,3,1024]{2,0,1:T(8,128)(2,1)}), bf16[1024,3,1024]{2,0,1:T(8,128)(2,1)}) %all-gather.3.cloned.1.call-update) | async-done | bytes 6291472 | tf_op jit(solution)/shard_map/all_gather | solution.py:20
  88.5 9.5 %convolution_convert_fusion = bf16[1024,3,768]{2,0,1:T(8,128)(2,1)} fusion(bf16[1024,3,1024]{2,0,1:T(8,128)(2,1)} %all-gather.3.cloned.1.call-done, bf16[768,1024]{1,0:T(8,128)(2,1)S(1)} %copy-done), kind=kOutput, calls=%fused_computation.2 | convolution fusion | flops 4834197504 | bytes 12582912 | tf_op jit(solution)/shard_map/td,csd->tsc/dot_general | solution.py:22
  98.1 6.7 %copy.21 = bf16[768,3072]{1,0:T(8,128)(2,1)} copy(bf16[768,3072]{0,1:T(8,128)(2,1)} %bitcast.69) | data formatting | bytes 9437184
  104.9 37.5 %reduce-scatter.7.cloned.1.call-done = bf16[96,3072]{1,0:T(8,128)(2,1)} async-done(((bf16[768,3072]{1,0:T(8,128)(2,1)}), bf16[96,3072]{1,0:T(8,128)(2,1)}) %reduce-scatter.7.cloned.1.call-update) | async-done | bytes 589840
  142.3 2.2 copy.22
  144.6 1.2 convert_element_type.30
  145.9 0.8 copy-done.1
  146.7 1.0 slice.147
  147.7 3.0 collective-permute-start
  150.7 1.1 copy.16
  151.8 5.3 %collective-permute-done = f32[6,1024]{0,1:T(8,128)} collective-permute-done((f32[6,1024]{0,1:T(8,128)}, f32[6,1024]{0,1:T(8,128)}, u32[]{:S(2)}, u32[]{:S(2)}) %collective-permute-start) | collective-permute-done | bytes 24608 | tf_op jit(solution)/shard_map/ppermute | solution.py:13
  157.1 6.9 %multiply_reduce_fusion = (f32[1024]{0:T(1024)S(1)}, f32[1024]{0:T(1024)S(1)}, f32[1024]{0:T(1024)S(1)}, f32[1024]{0:T(1024)S(1)}, f32[1024]{0:T(1024)S(1)}, /*i...) fusion(f32[96,1024]{0,1:T(8,128)} %copy-done.1, f32[6,1024]{0,1:T(8,128)} %collective-permute-done, ...), kind=kLoop, calls=%fused_computation.40 | loop fusion | flops 2155520 | bytes 1429504 | tf_op jit(solution)/shard_map/reduce_sum | solution.py:56
  164.0 1.9 collective-permute-start.1
  167.0 8.5 %collective-permute-done.1 = f32[6,1024]{0,1:T(8,128)} collective-permute-done((f32[6,1024]{0,1:T(8,128)}, f32[6,1024]{0,1:T(8,128)}, u32[]{:S(2)}, u32[]{:S(2)}) %collective-permute-start.1) | collective-permute-done | bytes 24608 | tf_op jit(solution)/shard_map/ppermute | solution.py:13
  175.6 10.0 %fusion.17 = (bf16[96,1,1024]{0,2,1:T(8,128)(2,1)S(1)}, f32[96,1024]{0,1:T(8,128)S(1)}, bf16[96,1,1024]{0,2,1:T(8,128)(2,1)S(1)}, f32[96,1024]{0,1:T(8,128)S(1)}) fusion(f32[96,3,1024]{0,2,1:T(8,128)S(1)} %convert_element_type.30, f32[6,1024]{0,1:T(8,128)} %collective-permute-done.1, f32[96,1024]{0,1:T(8,128)} %get-tuple-element.23, ...), kind=kLoop, calls=%fused_computation.52 | loop fusion | flops 4227072 | bytes 2633728 | tf_op jit(solution)/shard_map/stack | solution.py:52
  185.9 1.1 copy.17
  187.0 44.5 %all-gather.5.cloned.1.call-done = bf16[768,3,1024]{2,0,1:T(8,128)(2,1)} async-done(((bf16[96,3,1024]{2,0,1:T(8,128)(2,1)}), bf16[768,3,1024]{2,0,1:T(8,128)(2,1)}) %all-gather.5.cloned.1.call-update) | async-done | bytes 4718608 | tf_op jit(solution)/shard_map/all_gather | solution.py:59
  231.5 9.5 %convert_bitcast_fusion = bf16[1024,3,1024]{2,0,1:T(8,128)(2,1)} fusion(bf16[768,3,1024]{2,0,1:T(8,128)(2,1)} %all-gather.5.cloned.1.call-done, bf16[768,1024]{1,0:T(8,128)(2,1)S(1)} %copy-done), kind=kOutput, calls=%fused_computation | convolution fusion | flops 4834983936 | bytes 12582912 | tf_op jit(solution)/shard_map/tsc,td->csd/dot_general | solution.py:61
  241.2 9.4 %bitcast_convert_fusion = bf16[768,1024]{1,0:T(8,128)(2,1)} fusion(bf16[768,3,1024]{2,0,1:T(8,128)(2,1)} %all-gather.5.cloned.1.call-done, bf16[1024,3,1024]{2,0,1:T(8,128)(2,1)} %all-gather.3.cloned.1.call-done), kind=kOutput, calls=%fused_computation.1 | convolution fusion | flops 4832624640 | bytes 12582912 | tf_op jit(solution)/shard_map/tsc,csd->td/dot_general | solution.py:68
  252.0 149.2 %psum.15 = f32[7,64]{1,0:T(8,128)} all-reduce(f32[7,64]{1,0:T(8,128)S(1)} %stack.51), channel_id=1, replica_groups=mesh['row'=4,'col'=8,'depth'=8] {'col','depth'}, use_global_device_ids=true, to_apply=%region_17.0 | all-reduce | flops 448 | bytes 3584 | tf_op jit(solution)/shard_map/psum | solution.py:58
  401.2 0.8 copy.18
  402.0 2.5 convert_element_type.36
  404.5 2.7 copy.24
  (49 shorter events, 3.3 us)
Async XLA Ops:
  7.2 81.4 %copy-start = (bf16[768,1024]{1,0:T(8,128)(2,1)S(1)}, bf16[768,1024]{1,0:T(8,128)(2,1)}, u32[]{:S(2)}) copy-start(bf16[768,1024]{1,0:T(8,128)(2,1)} %param.4) | copy-start | bytes 4718596
  7.2 81.4 %all-gather.3.cloned.1.call-start = ((), (), s32[]{:S(2)}) async-start(), calls=%async_computation.2 | async-start | bytes 7077888 | tf_op jit(solution)/shard_map/all_gather | solution.py:20
  7.9 134.4 %reduce-scatter.7.cloned.1.call-start = ((), (), s32[]{:S(2)}) async-start(), calls=%async_computation.6 | async-start | bytes 5308416
  104.8 61.1 %copy-start.2 = (f32[7,64]{1,0:T(8,128)S(1)}, f32[7,64]{1,0:T(8,128)}, u32[]{:S(2)}) copy-start(f32[7,64]{1,0:T(8,128)} %param.6) | copy-start | bytes 5380
  104.8 126.7 %all-gather.5.cloned.1.call-start = ((), (), s32[]{:S(2)}) async-start(), calls=%async_computation.3 | async-start | bytes 5308416 | tf_op jit(solution)/shard_map/all_gather | solution.py:59
  145.9 0.8 copy-start.1
  147.7 9.4 %collective-permute-start = (f32[6,1024]{0,1:T(8,128)}, f32[6,1024]{0,1:T(8,128)}, u32[]{:S(2)}, u32[]{:S(2)}) collective-permute-start(f32[6,1024]{0,1:T(8,128)} %slice.147), channel_id=1, source_target_pairs={{0,1},{1,2},{2,3},{3,4},{4,5},{5,6},{6,7},{7,8},{8,9},{9,10},{10,1... | collective-permute-start | bytes 73736 | tf_op jit(solution)/shard_map/ppermute | solution.py:13
  164.0 11.6 %collective-permute-start.1 = (f32[6,1024]{0,1:T(8,128)}, f32[6,1024]{0,1:T(8,128)}, u32[]{:S(2)}, u32[]{:S(2)}) collective-permute-start(f32[6,1024]{0,1:T(8,128)} %bitcast.68), channel_id=1, source_target_pairs={{1,0},{2,1},{3,2},{4,3},{5,4},{6,5},{7,6},{8,7},{9,8},{10,9},{11,1... | collective-permute-start | bytes 73736 | tf_op jit(solution)/shard_map/ppermute | solution.py:13
  187.0 215.0 %reduce-scatter.5.cloned.1.call-start = ((), (), s32[]{:S(2)}) async-start(), calls=%async_computation.5 | async-start | bytes 7077888 | tf_op jit(solution)/shard_map/reduce_scatter | solution.py:60
  241.0 163.5 %all-reduce.2.cloned.1.call-start = ((), (), s32[]{:S(2)}) async-start(), calls=%async_computation.4 | async-start | bytes 3145728 | tf_op jit(solution)/shard_map/psum | solution.py:71
Sparse Core Ops, SparseCore 0:
  9.8 78.6 all-gather.2
  105.0 37.3 reduce-scatter.6
  187.1 44.3 all-gather.4
  241.1 75.6 reduce-scatter.4
  319.9 81.5 all-reduce.1
where the time goes:
time: 415 us; the launch traced here: 414 us
  waiting for transfers between devices  177 us (43%)
  blocking collectives  149 us (36%)
  matrix products  28.4 us (7%)
  other arithmetic  21.8 us (5%)
  local copies, waits for them, and re-layouts  18 us (4%)
  between operations  13.9 us (3%)
  starting transfers between devices  5.31 us (1%)
    psum x1, blocking collectives, on_device(): grad_taps = lax.psum(jnp.stack(tap_rows, 0), ('col', 'depth'))  149 us
    all_gather x1, waiting for transfers between devices, on_device(): panel_full = lax.all_gather(weight, 'col', axis=0, tiled=True)  80.6 us
    all_gather x1, waiting for transfers between devices, on_device(): grad_group = lax.all_gather(grad_proj, 'depth', axis=0, tiled=True)  44.5 us
    unnamed x6, waiting for transfers between devices  38.2 us
    unnamed x11, local copies, waits for them, and re-layouts  14.3 us
    ppermute x2, waiting for transfers between devices, passed_along(): lax.ppermute(value, axis, [(source, source + steps) for source in range(l...  13.8 us
    another operation x3, other arithmetic, on_device(): jnp.stack([grad_query, grad_key, grad_value], axis=1).astype(jnp.bfloat16)  10.3 us
    dot_general x1, matrix products, on_device(): jnp.einsum('td,csd->tsc', tokens, panel_full, preferred_element_type=jnp....  9.55 us
  transfers between devices with their start and end apart: 7, of which 5 were waited for; matrix products, arithmetic and copies ran while one was open for 4% of the time, Pallas kernels for 0%

commit v1 on v0

v1 whole, which is shorter than its diff:
```python
import jax
import jax.numpy as jnp
from jax import lax
from jax.experimental import pallas as pl
from jax.experimental.pallas import tpu as pltpu
from jax.sharding import PartitionSpec as P

MESH = pl.DeviceIdType.MESH
F32 = jnp.float32
BF16 = jnp.bfloat16
GROUP = 16
KT = 7
TOK = 768
ROWS = 96
CH = 128
SH = 3 * CH
DL = 1024
HALF = 512


def fma_dot(a, b, dims):
    return lax.dot_general(a, b, (dims, ((), ())), preferred_element_type=F32)


def kernel(
    tok_in, w_in, taps_ref, up_in,
    out_ref, gt_ref, gw_ref, ts_ref,
    T, W, U, PP, SB, S, R2, RM, RP, QKV, MX, GF, HM, HG, OB, G,
    TS, TR, TC, TY, TZ, PW, DR, DS, ES, ER, EO,
    l_sem, w_s, w_r, t_s, t_r, u_s, u_r, b_s, b_r, h_s, h_r, c_s, c_r,
    tr_s, tr_r, ty_s, ty_r, tz_s, tz_r, o_s, o_r, d_s, d_r, e_s, e_r, g_s, g_r,
):
    r, c, d = lax.axis_index("row"), lax.axis_index("col"), lax.axis_index("depth")
    zl, y, x, k = c // 4, c % 4, d // 2, d % 2
    z = 2 * r + zl

    def znb(delta):
        other = (z + delta + 8) % 8
        return (other // 2, (other % 2) * 4 + y, d)

    def ynb(delta):
        return (r, zl * 4 + (y + delta + 4) % 4, d)

    def xnb(delta):
        return (r, c, ((x + delta + 4) % 4) * 2 + k)

    def dnb(delta):
        return (r, c, (d + delta + 8) % 8)

    sib = (r, c, x * 2 + 1 - k)
    pair = (r, (1 - zl) * 4 + y, d)
    wraps_up = jnp.where(d == 7, 1, 0)
    wraps_down = jnp.where(d == 0, 1, 0)
    following = (r, zl * 4 + (y + wraps_up) % 4, (d + 1) % 8)
    previous = (r, zl * 4 + (y + 4 - wraps_down) % 4, (d + 7) % 8)

    def remote(src, dst, ssem, rsem, to):
        return pltpu.make_async_remote_copy(
            src_ref=src, dst_ref=dst, send_sem=ssem, recv_sem=rsem, device_id=to, device_id_type=MESH
        )

    sends = []

    def send(src, dst, ssem, rsem, to):
        copy = remote(src, dst, ssem, rsem, to)
        copy.start()
        sends.append(copy)

    def arrived(dst, rsem):
        remote(dst, dst, l_sem.at[0], rsem, sib).wait_recv()

    barrier = pltpu.get_barrier_semaphore()
    partners = [dnb(delta) for delta in range(1, 8)]
    partners += [ynb(delta) for delta in range(1, 4)]
    partners += [znb(delta) for delta in (1, -1, 2, -2)]
    partners += [following, previous]
    for partner in partners:
        pl.semaphore_signal(barrier, inc=1, device_id=partner, device_id_type=MESH)
    locals_ = [
        pltpu.make_async_copy(tok_in, T.at[0], l_sem.at[1]),
        pltpu.make_async_copy(w_in, W.at[y], l_sem.at[2]),
        pltpu.make_async_copy(
            up_in.at[:, pl.ds(pl.multiple_of(zl * HALF, HALF), HALF)], U.at[0], l_sem.at[3]
        ),
    ]
    for copy in locals_:
        copy.start()
    pl.semaphore_wait(barrier, len(partners))

    for first, way, side in ((0, 1, 0), (1, -1, 1)):
        for part in (first, 1 - first):
            send(w_in.at[part], W.at[y, part], w_s.at[side, part], w_r.at[side, part], ynb(way))
    send(tok_in.at[pl.ds(0, 384)], T.at[1, pl.ds(0, 384)], t_s.at[0], t_r.at[0], znb(-1))
    send(tok_in.at[pl.ds(384, 384)], T.at[1, pl.ds(384, 384)], t_s.at[1], t_r.at[1], znb(1))
    send(
        up_in.at[:, pl.ds(pl.multiple_of((1 - zl) * HALF, HALF), HALF)],
        U.at[1], u_s.at[0], u_r.at[0], pair,
    )
    for copy in locals_:
        copy.wait()

    def unit(u):
        i = u // 2
        return u % 2, (y + (i * (7 - i)) // 2) % 4

    def to_sibling(g, j):
        return remote(PP.at[g, j, :, 1 - k], SB.at[g, j], b_s.at[0, g, j], b_r.at[0, g, j], sib)

    def far(g, j):
        way = 1 - 2 * g
        return remote(S.at[g, j, (x + 2) % 4], R2.at[g, j], b_s.at[1, g, j], b_r.at[1, g, j], xnb(way))

    def back(g, j):
        way = 1 - 2 * g
        return remote(
            S.at[g, j, (x - way + 4) % 4], RM.at[g, j], b_s.at[2, g, j], b_r.at[2, g, j], xnb(-way)
        )

    def near(g, j):
        way = 1 - 2 * g
        return remote(
            S.at[g, j, (x + way + 4) % 4], RP.at[g, j], b_s.at[3, g, j], b_r.at[3, g, j], xnb(way)
        )

    def project(u):
        g, j = unit(u)
        part = fma_dot(T[g], W[j].reshape(SH, DL), ((1,), (1,)))
        PP[g, j] = part.astype(BF16).reshape(4, 2, ROWS, SH)
        to_sibling(g, j).start()

    def chip_sum(u):
        g, j = unit(u)
        to_sibling(g, j).wait_recv()
        for at in range(4):
            S[g, j, at] = (PP[g, j, at, k].astype(F32) + SB[g, j, at].astype(F32)).astype(BF16)
        far(g, j).start()
        back(g, j).start()

    def relay(u):
        g, j = unit(u)
        far(g, j).wait_recv()
        at = (x + 1 - 2 * g + 4) % 4
        S[g, j, at] = (S[g, j, at].astype(F32) + R2[g, j].astype(F32)).astype(BF16)
        near(g, j).start()

    def project_step(u, carry):
        @pl.when(u == 1)
        def _():
            chip_sum(0)
            arrived(W.at[(y + 3) % 4, 0], w_r.at[0, 0])
            remote(
                W.at[(y + 3) % 4, 0], W.at[(y + 3) % 4, 0], w_s.at[2, 0], w_r.at[2, 0], ynb(1)
            ).start()
            arrived(W.at[(y + 1) % 4, 1], w_r.at[1, 1])
            remote(
                W.at[(y + 1) % 4, 1], W.at[(y + 1) % 4, 1], w_s.at[2, 1], w_r.at[2, 1], ynb(-1)
            ).start()
            arrived(T.at[1, pl.ds(0, 384)], t_r.at[0])
            arrived(T.at[1, pl.ds(384, 384)], t_r.at[1])

        @pl.when(u == 2)
        def _():
            arrived(W.at[(y + 3) % 4, 1], w_r.at[0, 1])

        @pl.when(u == 4)
        def _():
            arrived(W.at[(y + 1) % 4, 0], w_r.at[1, 0])

        @pl.when(u == 6)
        def _():
            chip_sum(5)
            lax.fori_loop(0, 6, lambda v, unused: (relay(v), unused)[1], 0)
            arrived(W.at[(y + 2) % 4, 0], w_r.at[2, 0])
            arrived(W.at[(y + 2) % 4, 1], w_r.at[2, 1])

        project(u)

        @pl.when((u >= 2) & (u != 6))
        def _():
            chip_sum(u - 1)

        return carry

    lax.fori_loop(0, 8, project_step, 0)
    chip_sum(7)
    lax.fori_loop(6, 8, lambda v, unused: (relay(v), unused)[1], 0)
    arrived(U.at[1], u_r.at[0])

    def mixed_rows(j):
        return remote(MX.at[j, :, pl.ds(ROWS, 8)], HM.at[j], h_s.at[0, j], h_r.at[0, j], following)

    def grad_rows(j):
        return remote(GF.at[j, :, pl.ds(0, 8)], HG.at[j], h_s.at[1, j], h_r.at[1, j], previous)

    def total_step(i, carry):
        for g in range(2):
            _, j = unit(2 * i)
            back(g, j).wait_recv()
            near(g, j).wait_recv()
            total = S[g, j, x].astype(F32) + RM[g, j].astype(F32) + RP[g, j].astype(F32)
            total = total.astype(BF16).astype(F32)
            up = U[g, :, pl.ds(pl.multiple_of(j * CH, CH), CH)].astype(F32)
            QKV[g, j] = total
            MX[j, g, pl.ds(8, ROWS)] = total[:, CH : 2 * CH] * total[:, 2 * CH :]
            GF[j, g, pl.ds(0, ROWS)] = up * total[:, :CH]
        mixed_rows(j).start()
        grad_rows(j).start()
        return carry

    lax.fori_loop(0, 4, total_step, 0)

    def own_piece(g, j, way, at):
        return remote(
            G.at[g, j, x, k], G.at[g, j, x, k], c_s.at[at, g, j], c_r.at[at, g, j], xnb(way)
        )

    def relayed_piece(g, j):
        way = 1 - 2 * g
        at = (x - way + 4) % 4
        return remote(G.at[g, j, at, k], G.at[g, j, at, k], c_s.at[2, g, j], c_r.at[2, g, j], xnb(way))

    def to_sibling_back(g, j):
        return remote(G.at[g, j, :, k], G.at[g, j, :, k], c_s.at[3, g, j], c_r.at[3, g, j], sib)

    at_start = (y == 0) & (d == 0)
    at_end = (y == 3) & (d == 7)

    def halo_weights(edge, g, first):
        group = zl if g == 0 else 1 - zl
        same = jnp.where(edge, 0.0, 1.0)
        swapped = jnp.where(edge & (group == (1 if first else 0)), 1.0, 0.0)
        return same, swapped

    def filter_step(i, carry):
        _, j = unit(2 * i)
        mixed_rows(j).wait_recv()
        grad_rows(j).wait_recv()
        taps = taps_ref[zl * 4 + j]
        tap_sums = [None] * KT
        for g in range(2):
            same, swapped = halo_weights(at_start, g, True)
            MX[j, g, pl.ds(0, 8)] = HM[j, g] * same + HM[j, 1 - g] * swapped
            same, swapped = halo_weights(at_end, g, False)
            GF[j, g, pl.ds(ROWS, 8)] = HG[j, g] * same + HG[j, 1 - g] * swapped
            query = QKV[g, j, :, :CH]
            up = U[g, :, pl.ds(pl.multiple_of(j * CH, CH), CH)].astype(F32)
            grad = GF[j, g, pl.ds(0, ROWS)]
            filtered = jnp.zeros((ROWS, CH), F32)
            grad_mixed = jnp.zeros((ROWS, CH), F32)
            for o in range(KT):
                shifted = MX[j, g, pl.ds(8 - o, ROWS)]
                tap = taps[o : o + 1]
                filtered = filtered + tap * shifted
                grad_mixed = grad_mixed + tap * GF[j, g, pl.ds(o, ROWS)]
                summed = jnp.sum(grad * shifted, axis=0, keepdims=True)
                tap_sums[o] = summed if g == 0 else tap_sums[o] + summed
            gated = (query * filtered).astype(BF16)
            if g == 0:
                out_ref[:, pl.ds(pl.multiple_of((zl * 4 + j) * CH, CH), CH)] = gated
            else:
                OB[:, pl.ds(pl.multiple_of(j * CH, CH), CH)] = gated
            G[g, j, x, k, :, pl.ds(0, CH)] = (up * filtered).astype(BF16)
            G[g, j, x, k, :, pl.ds(CH, CH)] = (grad_mixed * QKV[g, j, :, 2 * CH :]).astype(BF16)
            G[g, j, x, k, :, pl.ds(2 * CH, CH)] = (grad_mixed * QKV[g, j, :, CH : 2 * CH]).astype(BF16)
            own_piece(g, j, 1, 0).start()
            own_piece(g, j, -1, 1).start()
        TS[j] = jnp.concatenate(tap_sums + [jnp.zeros((1, CH), F32)], axis=0)
        return carry

    lax.fori_loop(0, 4, filter_step, 0)

    def relay_piece_step(i, carry):
        _, j = unit(2 * i)
        own_piece(0, j, 1, 0).wait_recv()
        relayed_piece(0, j).start()
        own_piece(1, j, -1, 1).wait_recv()
        relayed_piece(1, j).start()
        return carry

    lax.fori_loop(0, 4, relay_piece_step, 0)

    def sibling_piece_step(i, carry):
        _, j = unit(2 * i)
        own_piece(0, j, -1, 1).wait_recv()
        own_piece(1, j, 1, 0).wait_recv()
        for g in range(2):
            relayed_piece(g, j).wait_recv()
            to_sibling_back(g, j).start()
        return carry

    lax.fori_loop(0, 4, sibling_piece_step, 0)
    send(
        OB, out_ref.at[:, pl.ds(pl.multiple_of(zl * HALF, HALF), HALF)], o_s.at[0], o_r.at[0], pair
    )
    for delta in range(1, 8):
        send(TS, TR.at[d], tr_s.at[delta], tr_r.at[d], dnb(delta))

    def gathered_step(i, carry):
        _, j = unit(2 * i)
        for g in range(2):
            to_sibling_back(g, j).wait_recv()
        return carry

    lax.fori_loop(0, 4, gathered_step, 0)

    def chunk(delta, side):
        group = abs(delta) % 2
        at = ((z + delta + 8) % 8) // 2
        total = None
        for j in range(4):
            rows = G[group, j, at].reshape(2 * ROWS, SH)
            columns = W[j, :, :, side * HALF : (side + 1) * HALF].reshape(SH, HALF)
            term = fma_dot(rows, columns, ((1,), (0,)))
            total = term if total is None else total + term
        return total

    def landed_chunk(way, steps, side):
        arrived(ER.at[way, steps, side], e_r.at[way, steps, side])
        return ER[way, steps, side].astype(F32)

    def send_chunk(way, steps, side, value):
        ES[way, steps, side] = value.astype(BF16)
        send(
            ES.at[way, steps, side], ER.at[way, steps, side],
            e_s.at[way, steps, side], e_r.at[way, steps, side], znb(1 - 2 * way),
        )

    def shard_grad(delta):
        j = (y + delta + 4) % 4
        total = None
        for g in range(2):
            term = fma_dot(G[g, j].reshape(TOK, SH), T[g], ((0,), (0,)))
            total = term if total is None else total + term
        return total

    def send_grad(way, kind, value):
        DS[way, kind] = value.astype(BF16)
        send(DS.at[way, kind], DR.at[way, kind], d_s.at[way, kind], d_r.at[way, kind], ynb(1 - 2 * way))

    def landed_grad(way, kind):
        arrived(DR.at[way, kind], d_r.at[way, kind])
        return DR[way, kind].astype(F32)

    cut = SH // 2
    send_chunk(0, 4, 0, chunk(4, 0))
    send_chunk(1, 4, 1, chunk(-4, 1))
    send_chunk(0, 3, 1, chunk(3, 1))
    send_chunk(1, 3, 0, chunk(-3, 0))
    part = shard_grad(2)
    send_grad(0, 0, part[:cut])
    send_grad(1, 0, part[cut:])
    send_chunk(0, 3, 0, chunk(3, 0) + landed_chunk(0, 4, 0))
    send_chunk(1, 3, 1, chunk(-3, 1) + landed_chunk(1, 4, 1))
    part = shard_grad(1)
    send_grad(0, 1, part[cut:])
    PW[0] = part[:cut]
    part = shard_grad(-1)
    send_grad(1, 1, part[:cut])
    PW[1] = part[cut:]
    send_chunk(0, 2, 1, chunk(2, 1) + landed_chunk(0, 3, 1))
    send_chunk(1, 2, 0, chunk(-2, 0) + landed_chunk(1, 3, 0))
    send_grad(0, 2, PW[0] + landed_grad(0, 0))
    send_grad(1, 2, PW[1] + landed_grad(1, 0))
    send_chunk(0, 2, 0, chunk(2, 0) + landed_chunk(0, 3, 0))
    send_chunk(1, 2, 1, chunk(-2, 1) + landed_chunk(1, 3, 1))

    TR[d] = TS[...]
    for delta in range(1, 8):
        source = (d + delta) % 8
        arrived(TR.at[source], tr_r.at[source])
    total = TR[0]
    for at in range(1, 8):
        total = total + TR[at]
    TC[...] = total
    TY[y] = total
    for delta in range(1, 4):
        send(TC, TY.at[y], ty_s.at[delta], ty_r.at[y], ynb(delta))

    send_chunk(0, 1, 1, chunk(1, 1) + landed_chunk(0, 2, 1))
    send_chunk(1, 1, 0, chunk(-1, 0) + landed_chunk(1, 2, 0))
    part = shard_grad(0)
    send_chunk(0, 1, 0, chunk(1, 0) + landed_chunk(0, 2, 0))
    send_chunk(1, 1, 1, chunk(-1, 1) + landed_chunk(1, 2, 1))
    gw_ref[...] = part

    for delta in range(1, 4):
        source = (y + delta) % 4
        arrived(TY.at[source], ty_r.at[source])
    total = TY[0]
    for at in range(1, 4):
        total = total + TY[at]
    TZ[...] = total
    ts_ref[zl] = total
    send(TZ, ts_ref.at[zl], tz_s.at[0], tz_r.at[0], pair)

    EO[1] = chunk(0, 1)
    EO[0] = chunk(0, 0)
    own_rows = pl.multiple_of(r * 2 * ROWS, 2 * ROWS)
    for side in (1, 0):
        columns = pl.ds(side * HALF, HALF)
        final = EO[side] + landed_chunk(0, 1, side) + landed_chunk(1, 1, side)
        gt_ref[pl.ds(own_rows, 2 * ROWS), columns] = final.astype(BF16)

    def final_rows(row, part):
        at = pl.multiple_of(((row + 4) % 4) * 2 * ROWS + part * ROWS, ROWS)
        return gt_ref.at[pl.ds(at, ROWS)]

    for part, way in ((0, 0), (1, 1), (1, 0), (0, 1)):
        rows = final_rows(r, part)
        send(rows, rows, g_s.at[way, part], g_r.at[way, part], znb(2 - 4 * way))
    for way in range(2):
        rows = final_rows(r - 1 + 2 * way, way)
        arrived(rows, g_r.at[way, way])
        send(rows, rows, g_s.at[2, way], g_r.at[2, way], znb(2 - 4 * way))

    for side in range(2):
        near_rows = pl.ds((1 - side) * cut, cut)
        mine = gw_ref[pl.ds(side * cut, cut)]
        if side == 0:
            mine = mine + landed_grad(0, 2) + landed_grad(1, 1)
        else:
            mine = mine + landed_grad(0, 1) + landed_grad(1, 2)
        gw_ref[pl.ds(side * cut, cut)] = mine

    arrived(final_rows(r - 1, 1), g_r.at[0, 1])
    arrived(final_rows(r + 1, 0), g_r.at[1, 0])
    arrived(final_rows(r + 2, 0), g_r.at[2, 0])
    arrived(final_rows(r + 2, 1), g_r.at[2, 1])
    arrived(ts_ref.at[1 - zl], tz_r.at[0])
    arrived(out_ref.at[:, pl.ds(pl.multiple_of((1 - zl) * HALF, HALF), HALF)], o_r.at[0])

    for copy in sends:
        copy.wait_send()
    for part, shard, way in ((0, 3, 1), (1, 1, -1)):
        rows = W.at[(y + shard) % 4, part]
        remote(rows, rows, w_s.at[2, part], w_r.at[2, part], ynb(way)).wait_send()

    def sent_step(j, carry):
        mixed_rows(j).wait_send()
        grad_rows(j).wait_send()
        for g in range(2):
            for copy in (to_sibling(g, j), far(g, j), back(g, j), near(g, j)):
                copy.wait_send()
            for copy in (
                own_piece(g, j, 1, 0), own_piece(g, j, -1, 1), relayed_piece(g, j), to_sibling_back(g, j)
            ):
                copy.wait_send()
        return carry

    lax.fori_loop(0, 4, sent_step, 0)


def on_device(tokens, weight, taps, upstream):
    shard = weight.transpose(1, 0, 2).reshape(2, SH // 2, DL)
    spread = jnp.repeat(taps, GROUP, axis=1)
    spread = jnp.concatenate([spread, jnp.zeros((1, spread.shape[1]), F32)], 0)
    spread = spread.reshape(8, 8, CH).transpose(1, 0, 2)
    vmem = pl.BlockSpec(memory_space=pltpu.VMEM)
    anywhere = pl.BlockSpec(memory_space=pl.ANY)
    dma = pltpu.SemaphoreType.DMA
    scratch = [
        pltpu.VMEM((2, TOK, DL), BF16),
        pltpu.VMEM((4, 2, SH // 2, DL), BF16),
        pltpu.VMEM((2, ROWS, HALF), BF16),
        pltpu.VMEM((2, 4, 4, 2, ROWS, SH), BF16),
        pltpu.VMEM((2, 4, 4, ROWS, SH), BF16),
        pltpu.VMEM((2, 4, 4, ROWS, SH), BF16),
        pltpu.VMEM((2, 4, ROWS, SH), BF16),
        pltpu.VMEM((2, 4, ROWS, SH), BF16),
        pltpu.VMEM((2, 4, ROWS, SH), BF16),
        pltpu.VMEM((2, 4, ROWS, SH), F32),
        pltpu.VMEM((4, 2, ROWS + 8, CH), F32),
        pltpu.VMEM((4, 2, ROWS + 8, CH), F32),
        pltpu.VMEM((4, 2, 8, CH), F32),
        pltpu.VMEM((4, 2, 8, CH), F32),
        pltpu.VMEM((ROWS, HALF), BF16),
        pltpu.VMEM((2, 4, 4, 2, ROWS, SH), BF16),
        pltpu.VMEM((4, 8, CH), F32),
        pltpu.VMEM((8, 4, 8, CH), F32),
        pltpu.VMEM((4, 8, CH), F32),
        pltpu.VMEM((4, 4, 8, CH), F32),
        pltpu.VMEM((4, 8, CH), F32),
        pltpu.VMEM((2, SH // 2, DL), F32),
        pltpu.VMEM((2, 3, SH // 2, DL), BF16),
        pltpu.VMEM((2, 3, SH // 2, DL), BF16),
        pltpu.VMEM((2, 5, 2, 2 * ROWS, HALF), BF16),
        pltpu.VMEM((2, 5, 2, 2 * ROWS, HALF), BF16),
        pltpu.VMEM((2, 2 * ROWS, HALF), F32),
        dma((4,)),
        dma((3, 2)), dma((3, 2)),
        dma((2,)), dma((2,)),
        dma((1,)), dma((1,)),
        dma((4, 2, 4)), dma((4, 2, 4)),
        dma((2, 4)), dma((2, 4)),
        dma((4, 2, 4)), dma((4, 2, 4)),
        dma((8,)), dma((8,)),
        dma((4,)), dma((4,)),
        dma((1,)), dma((1,)),
        dma((1,)), dma((1,)),
        dma((2, 3)), dma((2, 3)),
        dma((2, 5, 2)), dma((2, 5, 2)),
        dma((3, 2)), dma((3, 2)),
    ]
    output, grad_tokens, grad_weight, sums = pl.pallas_call(
        kernel,
        out_shape=(
            jax.ShapeDtypeStruct((ROWS, 2 * HALF), BF16),
            jax.ShapeDtypeStruct((TOK, DL), BF16),
            jax.ShapeDtypeStruct((SH, DL), F32),
            jax.ShapeDtypeStruct((2, 4, 8, CH), F32),
        ),
        in_specs=[anywhere, anywhere, vmem, anywhere],
        out_specs=(vmem, vmem, vmem, vmem),
        scratch_shapes=scratch,
        compiler_params=pltpu.CompilerParams(
            collective_id=0, has_side_effects=True, vmem_limit_bytes=58 * 1024 * 1024
        ),
        cost_estimate=pl.CostEstimate(
            flops=6 * TOK * DL * 8 * SH, bytes_accessed=8 * 1024 * 1024, transcendentals=0
        ),
    )(tokens, shard, spread, upstream)
    grad_weight = grad_weight.reshape(3, CH, DL).transpose(1, 0, 2)
    grad_taps = sums.reshape(8, 8, CH)[:, :KT].transpose(1, 0, 2).reshape(KT, -1, GROUP).sum(-1)
    return output, grad_tokens, grad_weight, grad_taps


def solution(mesh):
    in_specs = (
        P("col", "depth"),
        P(("row", "col"), None, "depth"),
        P(None, "row"),
        P(("col", "depth"), "row"),
    )
    out_specs = (
        P(("col", "depth"), "row"),
        P("col", "depth"),
        P(("row", "col"), None, "depth"),
        P(None, "row"),
    )
    return jax.shard_map(
        on_device, mesh=mesh, in_specs=in_specs, out_specs=out_specs, check_vma=False
    )
```

time: 415 us -> 153 us (0.37)
  waiting for transfers between devices: 177 us -> 0 us
  blocking collectives: 149 us -> 0 us
  Pallas kernels: 0 us -> 143 us
  matrix products: 28.4 us -> 0 us
  other arithmetic: 21.8 us -> 0.73 us
  between operations: 13.9 us -> 0.66 us
  local copies, waits for them, and re-layouts: 18 us -> 7.99 us
  starting transfers between devices: 5.31 us -> 0 us
    psum x1 -> x0, blocking collectives: 149 us -> none  [on_device(): grad_taps = lax.psum(jnp.stack(tap_rows, 0), ('col', 'depth'))]
    pallas_call x0 -> x1, Pallas kernels: none -> 143 us  [on_device(): pl.pallas_call(kernel, out_shape=(jax.ShapeDtypeStruct((ROWS, 2 * HALF),...]
    all_gather x2 -> x0, waiting for transfers between devices: 125 us -> none  [the longest x1 80.6 us: on_device(): panel_full = lax.all_gather(weight, 'col', axis=0, tiled=True)]
    unnamed x6 -> x0, waiting for transfers between devices: 38.2 us -> none
    dot_general x3 -> x0, matrix products: 28.4 us -> none  [the longest x1 9.55 us: on_device(): jnp.einsum('td,csd->tsc', tokens, panel_full, preferred_element_type=jnp....]
    ppermute x2 -> x0, waiting for transfers between devices: 13.8 us -> none  [passed_along(): lax.ppermute(value, axis, [(source, source + steps) for source in range(l...]
    another operation x3 -> x0, other arithmetic: 10.3 us -> none  [on_device(): jnp.stack([grad_query, grad_key, grad_value], axis=1).astype(jnp.bfloat16)]
    unnamed x11 -> x6, local copies, waits for them, and re-layouts: 14.3 us -> 6.31 us
  transfers between devices with their start and end apart: 7 -> 0, of which waited for: 5 -> 0; matrix products, arithmetic and copies ran while one was open for 4% -> 0% of each run, Pallas kernels for 0% -> 0%
where the time goes in v1:
time: 153 us
  Pallas kernels  143 us (93%)
  local copies, waits for them, and re-layouts  7.99 us (5%)
    pallas_call x1, Pallas kernels, on_device(): pl.pallas_call(kernel, out_shape=(jax.ShapeDtypeStruct((ROWS, 2 * HALF),...  143 us
    unnamed x6, local copies, waits for them, and re-layouts  6.31 us

profile of v1, /device:TPU:1, one launch (start us, length us, event | category | flops | bytes accessed | tf_op | source)
XLA Modules:
  0.0 152.6 jit_solution(3208516811358694663)
XLA Ops:
  0.6 0.8 broadcast_in_dim.4
  1.4 0.1 reshape.27
  1.6 0.6 pad_bitcast_fusion.taps_ref
  2.2 143.3 %shard_map.75 = (bf16[96,1024]{1,0:T(8,128)(2,1)}, bf16[768,1024]{1,0:T(8,128)(2,1)}, f32[384,1024]{1,0:T(8,128)}, f32[2,4,8,128]{3,2,1,0:T(8,128)}) custom-call(bf16[768,1024]{1,0:T(8,128)(2,1)} %tok_in.1, bf16[2,192,1024]{2,1,0:T(8,128)(2,1)} %bitcast.18, f32[8,8,128]{2,1,0:T(8,128)} %pad_bitcast_fusion.taps_ref, bf16[96,1024]{1,0:T(8,128)(2,1)} %up_in.1), custom_call_target="tpu_custom_call" | custom-call | flops 14495514624 | bytes 8388608 | tf_op jit(solution)/shard_map/pallas_call | solution.py:504
  145.5 0.8 copy.11
  146.2 0.1 reshape.31
  146.4 0.7 reduce_sum.9
  147.1 1.6 %copy.15 = bf16[96,1024]{1,0:T(8,128)(2,1)} copy(bf16[96,1024]{1,0:T(8,128)(2,1)} %get-tuple-element.16) | data formatting | bytes 393216
  148.7 0.0 copy-start
  148.7 2.8 %copy.16 = bf16[768,1024]{1,0:T(8,128)(2,1)} copy(bf16[768,1024]{1,0:T(8,128)(2,1)} %get-tuple-element.17) | data formatting | bytes 3145728
  151.5 0.0 copy-done
  151.5 1.1 copy.17
Async XLA Ops:
  148.7 2.8 %copy-start = (f32[384,1024]{1,0:T(8,128)S(1)}, f32[384,1024]{1,0:T(8,128)}, u32[]{:S(2)}) copy-start(f32[384,1024]{1,0:T(8,128)} %get-tuple-element.10) | copy-start | bytes 4718596

commit v2 on v1

v2 whole, which is shorter than its diff:
```python
import jax
import jax.numpy as jnp
from jax import lax
from jax.experimental import pallas as pl
from jax.experimental.pallas import tpu as pltpu
from jax.sharding import PartitionSpec as P

MESH = pl.DeviceIdType.MESH
F32 = jnp.float32
BF16 = jnp.bfloat16
GROUP = 16
KT = 7
TOK = 768
ROWS = 96
CH = 128
SH = 3 * CH
DL = 1024
HALF = 512
QUARTER = 256


def fma_dot(a, b, dims):
    return lax.dot_general(a, b, (dims, ((), ())), preferred_element_type=F32)


def group_of_channel(channel_axis):
    shape = (2 * HALF // GROUP, 2 * HALF) if channel_axis == 0 else (2 * HALF, 2 * HALF // GROUP)
    groups = lax.broadcasted_iota(jnp.int32, shape, channel_axis)
    channels = lax.broadcasted_iota(jnp.int32, shape, 1 - channel_axis)
    return jnp.where(channels // GROUP == groups, 1.0, 0.0)


def kernel(
    tok_in, w_in, taps_ref, up_in,
    out_ref, gt_ref, gw_ref, ts_ref,
    T, W, SP, U, PP, SB, S, R2, RM, RP, QKV, MX, GF, HM, HG, OB, G,
    TS, TR, TC, TY, TZ, TO, PW, DR, DS, GW, EP, ES, ER, FV,
    l_sem, w_s, w_r, t_s, t_r, u_s, u_r, b_s, b_r, h_s, h_r, c_s, c_r,
    tr_s, tr_r, ty_s, ty_r, tz_s, tz_r, o_s, o_r, d_s, d_r, e_s, e_r, g_s, g_r, f_sem,
):
    r, c, d = lax.axis_index("row"), lax.axis_index("col"), lax.axis_index("depth")
    zl, y, x, k = c // 4, c % 4, d // 2, d % 2
    z = 2 * r + zl

    def znb(delta):
        other = (z + delta + 8) % 8
        return (other // 2, (other % 2) * 4 + y, d)

    def ynb(delta):
        return (r, zl * 4 + (y + delta + 4) % 4, d)

    def xnb(delta):
        return (r, c, ((x + delta + 4) % 4) * 2 + k)

    def dnb(delta):
        return (r, c, (d + delta + 8) % 8)

    sib = (r, c, x * 2 + 1 - k)
    pair = (r, (1 - zl) * 4 + y, d)
    wraps_up = jnp.where(d == 7, 1, 0)
    wraps_down = jnp.where(d == 0, 1, 0)
    following = (r, zl * 4 + (y + wraps_up) % 4, (d + 1) % 8)
    previous = (r, zl * 4 + (y + 4 - wraps_down) % 4, (d + 7) % 8)

    def remote(src, dst, ssem, rsem, to):
        return pltpu.make_async_remote_copy(
            src_ref=src, dst_ref=dst, send_sem=ssem, recv_sem=rsem, device_id=to, device_id_type=MESH
        )

    sends = []

    def send(src, dst, ssem, rsem, to):
        copy = remote(src, dst, ssem, rsem, to)
        copy.start()
        sends.append(copy)

    def arrived(dst, rsem):
        remote(dst, dst, l_sem.at[0], rsem, sib).wait_recv()

    def each(start, stop, step):
        def body(at, carry):
            step(at)
            return carry

        lax.fori_loop(start, stop, body, 0)

    def lanes(at, width):
        return pl.ds(pl.multiple_of(at * width, width), width)

    barrier = pltpu.get_barrier_semaphore()
    partners = [dnb(delta) for delta in range(1, 8)]
    partners += [ynb(delta) for delta in range(1, 4)]
    partners += [znb(delta) for delta in (1, -1, 2, -2)]
    partners += [following, previous]
    for partner in partners:
        pl.semaphore_signal(barrier, inc=1, device_id=partner, device_id_type=MESH)
    locals_ = [
        pltpu.make_async_copy(tok_in, T.at[zl], l_sem.at[1]),
        pltpu.make_async_copy(w_in, W.at[y], l_sem.at[2]),
        pltpu.make_async_copy(up_in.at[:, lanes(zl, HALF)], U.at[zl], l_sem.at[3]),
    ]
    for copy in locals_:
        copy.start()
    pl.semaphore_wait(barrier, len(partners))

    for first, way, side in ((0, 1, 0), (1, -1, 1)):
        for part in (first, 1 - first):
            send(w_in.at[part], W.at[y, part], w_s.at[side, part], w_r.at[side, part], ynb(way))
    send(tok_in.at[pl.ds(0, 384)], T.at[zl, pl.ds(0, 384)], t_s.at[0], t_r.at[0], znb(-1))
    send(tok_in.at[pl.ds(384, 384)], T.at[zl, pl.ds(384, 384)], t_s.at[1], t_r.at[1], znb(1))
    send(up_in.at[:, lanes(1 - zl, HALF)], U.at[zl], u_s.at[0], u_r.at[0], pair)
    for copy in locals_:
        copy.wait()
    spread = lax.dot_general(
        taps_ref[...], group_of_channel(0), (((1,), (0,)), ((), ())), precision=lax.Precision.HIGHEST,
        preferred_element_type=F32,
    )
    for at in range(8):
        SP[at, pl.ds(0, KT)] = spread[:, at * CH : (at + 1) * CH]

    def shard_at(i):
        return (y + (i * (7 - i)) // 2) % 4

    def unit(u):
        return (u + zl) % 2, shard_at(u // 2), 1 - 2 * (u % 2)

    def to_sibling(g, j):
        return remote(PP.at[g, j, :, 1 - k], SB.at[g, j], b_s.at[0, g, j], b_r.at[0, g, j], sib)

    def far(g, j, way):
        return remote(S.at[g, j, (x + 2) % 4], R2.at[g, j], b_s.at[1, g, j], b_r.at[1, g, j], xnb(way))

    def back(g, j, way):
        return remote(
            S.at[g, j, (x - way + 4) % 4], RM.at[g, j], b_s.at[2, g, j], b_r.at[2, g, j], xnb(-way)
        )

    def near(g, j, way):
        return remote(
            S.at[g, j, (x + way + 4) % 4], RP.at[g, j], b_s.at[3, g, j], b_r.at[3, g, j], xnb(way)
        )

    def project(u):
        g, j, _ = unit(u)
        part = fma_dot(T[g], W[j].reshape(SH, DL), ((1,), (1,)))
        PP[g, j] = part.astype(BF16).reshape(4, 2, ROWS, SH)
        to_sibling(g, j).start()

    def chip_sum(u):
        g, j, way = unit(u)
        to_sibling(g, j).wait_recv()
        for at in range(4):
            S[g, j, at] = (PP[g, j, at, k].astype(F32) + SB[g, j, at].astype(F32)).astype(BF16)
        far(g, j, way).start()
        back(g, j, way).start()

    def relay(u):
        g, j, way = unit(u)
        far(g, j, way).wait_recv()
        at = (x + way + 4) % 4
        S[g, j, at] = (S[g, j, at].astype(F32) + R2[g, j].astype(F32)).astype(BF16)
        near(g, j, way).start()

    def relayed_weights(part):
        way = 1 - 2 * part
        rows = W.at[(y - way + 4) % 4, part]
        return remote(rows, rows, w_s.at[2, part], w_r.at[2, part], ynb(way))

    def project_step(u):
        @pl.when(u == 1)
        def _():
            chip_sum(0)
            arrived(W.at[(y + 3) % 4, 0], w_r.at[0, 0])
            relayed_weights(0).start()
            arrived(W.at[(y + 1) % 4, 1], w_r.at[1, 1])
            relayed_weights(1).start()
            relay(0)
            arrived(T.at[1 - zl, pl.ds(0, 384)], t_r.at[0])
            arrived(T.at[1 - zl, pl.ds(384, 384)], t_r.at[1])

        @pl.when(u == 2)
        def _():
            arrived(W.at[(y + 3) % 4, 1], w_r.at[0, 1])

        @pl.when(u == 4)
        def _():
            arrived(W.at[(y + 1) % 4, 0], w_r.at[1, 0])

        @pl.when(u == 6)
        def _():
            chip_sum(5)
            arrived(W.at[(y + 2) % 4, 0], w_r.at[2, 0])
            arrived(W.at[(y + 2) % 4, 1], w_r.at[2, 1])

        project(u)

        @pl.when((u >= 2) & (u != 6))
        def _():
            chip_sum(u - 1)

        @pl.when(u >= 4)
        def _():
            relay(u - 3)

    each(0, 8, project_step)
    chip_sum(7)
    relay(5)

    def mixed_rows(j):
        return remote(MX.at[j, :, pl.ds(ROWS, 8)], HM.at[j], h_s.at[0, j], h_r.at[0, j], following)

    def grad_rows(j):
        return remote(GF.at[j, :, pl.ds(0, 8)], HG.at[j], h_s.at[1, j], h_r.at[1, j], previous)

    def total_step(i):
        for half in range(2):
            g, j, way = unit(2 * i + half)
            back(g, j, way).wait_recv()
            near(g, j, way).wait_recv()
            total = S[g, j, x].astype(F32) + RM[g, j].astype(F32) + RP[g, j].astype(F32)
            total = total.astype(BF16).astype(F32)
            up = U[g, :, lanes(j, CH)].astype(F32)
            QKV[g, j] = total
            MX[j, g, pl.ds(8, ROWS)] = total[:, CH : 2 * CH] * total[:, 2 * CH :]
            GF[j, g, pl.ds(0, ROWS)] = up * total[:, :CH]
        mixed_rows(j).start()
        grad_rows(j).start()

    arrived(U.at[1 - zl], u_r.at[0])
    each(0, 3, total_step)
    each(6, 8, relay)
    each(3, 4, total_step)

    def own_piece(g, j, to_left):
        rows = G.at[g, x, k, :, lanes(j, SH)]
        return remote(rows, rows, c_s.at[to_left, g, j], c_r.at[to_left, g, j], xnb(1 - 2 * to_left))

    def relayed_piece(g, j, to_left):
        way = 1 - 2 * to_left
        rows = G.at[g, (x - way + 4) % 4, k, :, lanes(j, SH)]
        return remote(rows, rows, c_s.at[2, g, j], c_r.at[2, g, j], xnb(way))

    def to_sibling_back(g, j):
        rows = G.at[g, :, k, :, lanes(j, SH)]
        return remote(rows, rows, c_s.at[3, g, j], c_r.at[3, g, j], sib)

    def filter_step(g, i):
        j = shard_at(i)
        if g == 0:
            mixed_rows(j).wait_recv()
            grad_rows(j).wait_recv()
        at_start = (y == 0) & (d == 0)
        at_end = (y == 3) & (d == 7)
        same = jnp.where(at_start, 0.0, 1.0)
        swapped = jnp.where(at_start, 1.0 * g, 0.0)
        MX[j, g, pl.ds(0, 8)] = HM[j, g] * same + HM[j, 1 - g] * swapped
        same = jnp.where(at_end, 0.0, 1.0)
        swapped = jnp.where(at_end, 1.0 - g, 0.0)
        GF[j, g, pl.ds(ROWS, 8)] = HG[j, g] * same + HG[j, 1 - g] * swapped
        taps = SP[zl * 4 + j]
        query = QKV[g, j, :, :CH]
        up = U[g, :, lanes(j, CH)].astype(F32)
        grad = GF[j, g, pl.ds(0, ROWS)]
        filtered = jnp.zeros((ROWS, CH), F32)
        grad_mixed = jnp.zeros((ROWS, CH), F32)
        tap_sums = []
        for o in range(KT):
            shifted = MX[j, g, pl.ds(8 - o, ROWS)]
            tap = taps[o : o + 1]
            filtered = filtered + tap * shifted
            grad_mixed = grad_mixed + tap * GF[j, g, pl.ds(o, ROWS)]
            tap_sums.append(jnp.sum(grad * shifted, axis=0, keepdims=True))
        OB[g, :, lanes(j, CH)] = (query * filtered).astype(BF16)
        G[g, x, k, :, lanes(3 * j, CH)] = (up * filtered).astype(BF16)
        G[g, x, k, :, lanes(3 * j + 1, CH)] = (grad_mixed * QKV[g, j, :, 2 * CH :]).astype(BF16)
        G[g, x, k, :, lanes(3 * j + 2, CH)] = (grad_mixed * QKV[g, j, :, CH : 2 * CH]).astype(BF16)
        TS[g, j] = jnp.concatenate(tap_sums + [jnp.zeros((1, CH), F32)], axis=0)

        own_piece(g, j, 0).start()
        own_piece(g, j, 1).start()

    def relay_piece(g, i):
        j, to_left = shard_at(i), i % 2
        own_piece(g, j, to_left).wait_recv()
        relayed_piece(g, j, to_left).start()

    def sibling_piece(g, i):
        j, to_left = shard_at(i), i % 2
        own_piece(g, j, 1 - to_left).wait_recv()
        relayed_piece(g, j, to_left).wait_recv()
        to_sibling_back(g, j).start()

    def gathered(g, i):
        to_sibling_back(g, shard_at(i)).wait_recv()

    def second_group(i):
        filter_step(1, i)
        sibling_piece(0, i)

    each(0, 4, lambda i: filter_step(0, i))
    each(0, 4, lambda i: relay_piece(0, i))
    each(0, 4, second_group)
    send(OB.at[1 - zl], out_ref.at[:, lanes(zl, HALF)], o_s.at[0], o_r.at[0], pair)
    out_copy = pltpu.make_async_copy(OB.at[zl], out_ref.at[:, lanes(zl, HALF)], l_sem.at[4])
    out_copy.start()
    TC[...] = TS[0] + TS[1]
    for delta in range(1, 8):
        send(TC, TR.at[d], tr_s.at[delta], tr_r.at[d], dnb(delta))
    TR[d] = TC[...]
    each(0, 4, lambda i: gathered(0, i))

    def own_chunk(g, delta, piece):
        return EP[g, piece, lanes(((z + delta + 8) % 8) // 2, 2 * ROWS)]

    def chunk_copy(way, steps, piece):
        return remote(
            ES.at[way, steps, piece], ER.at[way, steps, piece],
            e_s.at[way, steps, piece], e_r.at[way, steps, piece], znb(1 - 2 * way),
        )

    def landed_chunk(way, steps, piece):
        chunk_copy(way, steps, piece).wait_recv()
        return ER[way, steps, piece].astype(F32)

    def send_chunk(g, way, steps, piece, received):
        value = own_chunk(g, steps * (1 - 2 * way), piece)
        if received:
            value = value + landed_chunk(way, steps + 1, piece)
        ES[way, steps, piece] = value.astype(BF16)
        chunk_copy(way, steps, piece).start()

    def token_grads(g, start, stop):
        def step(side):
            both = fma_dot(
                G[g].reshape(TOK, 4 * SH), W[:, :, :, lanes(side, HALF)].reshape(4 * SH, HALF), ((1,), (0,))
            )
            EP[g, 2 * side] = both[:, :QUARTER]
            EP[g, 2 * side + 1] = both[:, QUARTER:]

            @pl.when((zl == g) & (side == 0))
            def _():
                send_chunk(g, 0, 4, 0, False)
                send_chunk(g, 0, 4, 1, False)

            @pl.when((zl == g) & (side == 1))
            def _():
                send_chunk(g, 1, 4, 3, False)
                send_chunk(g, 1, 4, 2, False)

            @pl.when((zl != g) & (side == 0))
            def _():
                send_chunk(g, 1, 3, 1, False)
                send_chunk(g, 1, 3, 0, False)

            @pl.when((zl != g) & (side == 1))
            def _():
                send_chunk(g, 0, 3, 2, False)
                send_chunk(g, 0, 3, 3, False)

        each(start, stop, step)

    def ring_step(g, owner, steps, start, stop):
        @pl.when((zl == g) == owner)
        def _():
            def step(at):
                piece = (at + 2) % 4
                send_chunk(g, 0, steps, piece, True)
                send_chunk(g, 1, steps, 3 - piece, True)

            each(start, stop, step)

    def final_rows(row, piece):
        return gt_ref.at[lanes((row + 4) % 4, 2 * ROWS), lanes(piece, QUARTER)]

    def final_copy(piece, way):
        return remote(
            FV.at[piece], final_rows(r, piece), g_s.at[way, piece], g_r.at[way, piece], znb(2 - 4 * way)
        )

    def final_relay(piece):
        way = piece % 2
        rows = final_rows(r - 1 + 2 * way, piece)
        return remote(rows, rows, g_s.at[2, piece], g_r.at[2, piece], znb(2 - 4 * way))

    def final_own(piece):
        return pltpu.make_async_copy(FV.at[piece], final_rows(r, piece), f_sem.at[piece])

    def finish(g, start, stop):
        @pl.when(zl == g)
        def _():
            def step(at):
                piece = (at + 2) % 4
                total = own_chunk(g, 0, piece) + landed_chunk(0, 1, piece) + landed_chunk(1, 1, piece)
                FV[piece] = total.astype(BF16)
                final_copy(piece, 0).start()
                final_copy(piece, 1).start()
                final_own(piece).start()

            each(start, stop, step)

    def finish_relay(g, start, stop):
        @pl.when(zl == g)
        def _():
            def step(at):
                piece = (at + 2) % 4
                way = piece % 2
                arrived(final_rows(r - 1 + 2 * way, piece), g_r.at[way, piece])
                final_relay(piece).start()

            each(start, stop, step)

    def shard_grad(delta):
        j = (y + delta + 4) % 4
        total = None
        for g in range(2):
            term = fma_dot(G[g, :, :, :, lanes(j, SH)].reshape(TOK, SH), T[g], ((0,), (0,)))
            total = term if total is None else total + term
        return total

    def send_grad(way, kind, value):
        DS[way, kind] = value.astype(BF16)
        send(DS.at[way, kind], DR.at[way, kind], d_s.at[way, kind], d_r.at[way, kind], ynb(1 - 2 * way))

    def landed_grad(way, kind):
        arrived(DR.at[way, kind], d_r.at[way, kind])
        return DR[way, kind].astype(F32)

    cut = SH // 2
    token_grads(0, 0, 2)
    each(0, 4, lambda i: relay_piece(1, i))
    ring_step(0, False, 3, 2, 4)
    ring_step(0, True, 2, 0, 2)
    each(0, 4, lambda i: sibling_piece(1, i))
    each(0, 4, lambda i: gathered(1, i))
    token_grads(1, 0, 1)
    ring_step(0, True, 2, 2, 4)
    token_grads(1, 1, 2)
    ring_step(0, False, 1, 0, 2)
    ring_step(1, False, 3, 2, 4)
    ring_step(0, False, 1, 2, 4)
    part = shard_grad(2)
    send_grad(0, 0, part[:cut])
    send_grad(1, 0, part[cut:])
    ring_step(1, True, 2, 0, 2)
    ring_step(1, True, 2, 2, 4)
    part = shard_grad(1)
    send_grad(0, 1, part[cut:])
    PW[0] = part[:cut]
    ring_step(1, False, 1, 0, 2)
    ring_step(1, False, 1, 2, 4)
    finish(0, 0, 4)
    finish(1, 0, 4)
    part = shard_grad(-1)
    send_grad(1, 1, part[:cut])
    PW[1] = part[cut:]

    for delta in range(1, 8):
        source = (d + delta) % 8
        arrived(TR.at[source], tr_r.at[source])
    total = TR[0]
    for at in range(1, 8):
        total = total + TR[at]
    TZ[...] = total
    TY[y] = total
    for delta in range(1, 4):
        send(TZ, TY.at[y], ty_s.at[delta], ty_r.at[y], ynb(delta))

    send_grad(0, 2, PW[0] + landed_grad(0, 0))
    send_grad(1, 2, PW[1] + landed_grad(1, 0))
    finish_relay(0, 0, 4)
    finish_relay(1, 0, 4)
    GW[...] = shard_grad(0)

    for delta in range(1, 4):
        source = (y + delta) % 4
        arrived(TY.at[source], ty_r.at[source])
    total = TY[0]
    for at in range(1, 4):
        total = total + TY[at]
    TO[zl] = total
    send(TO.at[zl], TO.at[zl], tz_s.at[0], tz_r.at[0], pair)

    GW[pl.ds(0, cut)] = GW[pl.ds(0, cut)] + landed_grad(0, 2) + landed_grad(1, 1)
    GW[pl.ds(cut, cut)] = GW[pl.ds(cut, cut)] + landed_grad(0, 1) + landed_grad(1, 2)
    gw_copy = pltpu.make_async_copy(GW, gw_ref, l_sem.at[5])
    gw_copy.start()

    arrived(TO.at[1 - zl], tz_r.at[0])
    sums = jnp.concatenate([TO[at // 4, at % 4] for at in range(8)], axis=1)
    ts_ref[...] = lax.dot_general(
        sums, group_of_channel(1), (((1,), (0,)), ((), ())), precision=lax.Precision.HIGHEST,
        preferred_element_type=F32,
    )[:KT]
    arrived(out_ref.at[:, lanes(1 - zl, HALF)], o_r.at[0])
    for piece in range(4):
        way = piece % 2
        arrived(final_rows(r + 1 - 2 * way, piece), g_r.at[1 - way, piece])
        arrived(final_rows(r + 2, piece), g_r.at[2, piece])
        final_own(piece).wait()
    out_copy.wait()
    gw_copy.wait()

    for copy in sends:
        copy.wait_send()
    for part in range(2):
        relayed_weights(part).wait_send()

    def sent_piece(piece):
        final_relay(piece).wait_send()
        for way in range(2):
            final_copy(piece, way).wait_send()
            for steps in range(1, 4):
                chunk_copy(way, steps, piece).wait_send()
        chunk_copy(piece // 2, 4, piece).wait_send()

    each(0, 4, sent_piece)

    def sent_step(u):
        g, j, way = unit(u)

        @pl.when(u % 2 == 0)
        def _():
            mixed_rows(j).wait_send()
            grad_rows(j).wait_send()

        for copy in (to_sibling(g, j), far(g, j, way), back(g, j, way), near(g, j, way)):
            copy.wait_send()
        for copy in (
            own_piece(g, j, 0), own_piece(g, j, 1), relayed_piece(g, j, (u // 2) % 2), to_sibling_back(g, j)
        ):
            copy.wait_send()

    each(0, 8, sent_step)


def hand_over(out_in, gt_in, gw_in, taps_in, out_ref, gt_ref, gw_ref, taps_ref, out_v, gt_v, gw_v, sem):
    steps = []
    for src, held, dst, parts in ((gt_in, gt_v, gt_ref, 4), (gw_in, gw_v, gw_ref, 4), (out_in, out_v, out_ref, 1)):
        rows = held.shape[0] // parts
        for part in range(parts):
            at = pl.ds(part * rows, rows)
            steps.append((src.at[at], held.at[at], dst.at[at]))
    reads = [pltpu.make_async_copy(src, held, sem.at[0, n]) for n, (src, held, _) in enumerate(steps)]
    writes = [pltpu.make_async_copy(held, dst, sem.at[1, n]) for n, (_, held, dst) in enumerate(steps)]
    for copy in reads:
        copy.start()
    taps_ref[...] = taps_in[...]
    for read, write in zip(reads, writes):
        read.wait()
        write.start()
    for copy in writes:
        copy.wait()


def on_device(tokens, weight, taps, upstream):
    shard = weight.transpose(1, 0, 2).reshape(2, SH // 2, DL)
    vmem = pl.BlockSpec(memory_space=pltpu.VMEM)
    anywhere = pl.BlockSpec(memory_space=pl.ANY)
    dma = pltpu.SemaphoreType.DMA
    scratch = [
        pltpu.VMEM((2, TOK, DL), BF16),
        pltpu.VMEM((4, 2, SH // 2, DL), BF16),
        pltpu.VMEM((8, 8, CH), F32),
        pltpu.VMEM((2, ROWS, HALF), BF16),
        pltpu.VMEM((2, 4, 4, 2, ROWS, SH), BF16),
        pltpu.VMEM((2, 4, 4, ROWS, SH), BF16),
        pltpu.VMEM((2, 4, 4, ROWS, SH), BF16),
        pltpu.VMEM((2, 4, ROWS, SH), BF16),
        pltpu.VMEM((2, 4, ROWS, SH), BF16),
        pltpu.VMEM((2, 4, ROWS, SH), BF16),
        pltpu.VMEM((2, 4, ROWS, SH), F32),
        pltpu.VMEM((4, 2, ROWS + 8, CH), F32),
        pltpu.VMEM((4, 2, ROWS + 8, CH), F32),
        pltpu.VMEM((4, 2, 8, CH), F32),
        pltpu.VMEM((4, 2, 8, CH), F32),
        pltpu.VMEM((2, ROWS, HALF), BF16),
        pltpu.VMEM((2, 4, 2, ROWS, 4 * SH), BF16),
        pltpu.VMEM((2, 4, 8, CH), F32),
        pltpu.VMEM((8, 4, 8, CH), F32),
        pltpu.VMEM((4, 8, CH), F32),
        pltpu.VMEM((4, 4, 8, CH), F32),
        pltpu.VMEM((4, 8, CH), F32),
        pltpu.VMEM((2, 4, 8, CH), F32),
        pltpu.VMEM((2, SH // 2, DL), F32),
        pltpu.VMEM((2, 3, SH // 2, DL), BF16),
        pltpu.VMEM((2, 3, SH // 2, DL), BF16),
        pltpu.VMEM((SH, DL), F32),
        pltpu.VMEM((2, 4, TOK, QUARTER), F32),
        pltpu.VMEM((2, 5, 4, 2 * ROWS, QUARTER), BF16),
        pltpu.VMEM((2, 5, 4, 2 * ROWS, QUARTER), BF16),
        pltpu.VMEM((4, 2 * ROWS, QUARTER), BF16),
        dma((6,)),
        dma((3, 2)), dma((3, 2)),
        dma((2,)), dma((2,)),
        dma((1,)), dma((1,)),
        dma((4, 2, 4)), dma((4, 2, 4)),
        dma((2, 4)), dma((2, 4)),
        dma((4, 2, 4)), dma((4, 2, 4)),
        dma((8,)), dma((8,)),
        dma((4,)), dma((4,)),
        dma((1,)), dma((1,)),
        dma((1,)), dma((1,)),
        dma((2, 3)), dma((2, 3)),
        dma((2, 5, 4)), dma((2, 5, 4)),
        dma((3, 4)), dma((3, 4)),
        dma((4,)),
    ]
    shapes = (
        jax.ShapeDtypeStruct((ROWS, 2 * HALF), BF16),
        jax.ShapeDtypeStruct((TOK, DL), BF16),
        jax.ShapeDtypeStruct((SH, DL), F32),
        jax.ShapeDtypeStruct((KT, 2 * HALF // GROUP), F32),
    )
    results = pl.pallas_call(
        kernel,
        out_shape=tuple(pltpu.VMEM(shape.shape, shape.dtype) for shape in shapes),
        in_specs=[anywhere, anywhere, vmem, anywhere],
        out_specs=(vmem, vmem, vmem, vmem),
        scratch_shapes=scratch,
        compiler_params=pltpu.CompilerParams(
            collective_id=0, has_side_effects=True, vmem_limit_bytes=58 * 1024 * 1024
        ),
        cost_estimate=pl.CostEstimate(
            flops=6 * TOK * DL * 8 * SH, bytes_accessed=8 * 1024 * 1024, transcendentals=0
        ),
    )(tokens, shard, taps, upstream)
    output, grad_tokens, grad_weight, grad_taps = results
    grad_weight = grad_weight.reshape(3, CH, DL).transpose(1, 0, 2)
    return output, grad_tokens, grad_weight, grad_taps


def solution(mesh):
    in_specs = (
        P("col", "depth"),
        P(("row", "col"), None, "depth"),
        P(None, "row"),
        P(("col", "depth"), "row"),
    )
    out_specs = (
        P(("col", "depth"), "row"),
        P("col", "depth"),
        P(("row", "col"), None, "depth"),
        P(None, "row"),
    )
    return jax.shard_map(
        on_device, mesh=mesh, in_specs=in_specs, out_specs=out_specs, check_vma=False
    )
```

time: 153 us -> 145 us (0.948)
  local copies, waits for them, and re-layouts: 7.99 us -> 3.56 us
  Pallas kernels: 143 us -> 139 us
    pallas_call x1, Pallas kernels: 143 us -> 139 us  [on_device(): pl.pallas_call(kernel, out_shape=tuple((pltpu.VMEM(shape.shape, shape.dty...]
    unnamed x6 -> x4, local copies, waits for them, and re-layouts: 6.31 us -> 3.56 us
where the time goes in v2:
time: 145 us; the launch traced here: 144 us
  Pallas kernels  139 us (96%)
  local copies, waits for them, and re-layouts  3.56 us (2%)
    pallas_call x1, Pallas kernels, on_device(): pl.pallas_call(kernel, out_shape=tuple((pltpu.VMEM(shape.shape, shape.dty...  139 us
    unnamed x4, local copies, waits for them, and re-layouts  3.56 us

profile of v2, /device:TPU:1, one launch (start us, length us, event | category | flops | bytes accessed | tf_op | source)
XLA Modules:
  0.0 143.6 jit_solution(2549671641714014788)
XLA Ops:
  0.6 139.4 %shard_map.75 = (bf16[96,1024]{1,0:T(8,128)(2,1)S(1)}, bf16[768,1024]{1,0:T(8,128)(2,1)S(1)}, f32[384,1024]{1,0:T(8,128)S(1)}, f32[7,64]{1,0:T(8,128)S(1)}) custom-call(bf16[768,1024]{1,0:T(8,128)(2,1)} %tok_in.1, bf16[2,192,1024]{2,1,0:T(8,128)(2,1)} %bitcast.7, f32[7,64]{1,0:T(8,128)} %taps_ref.1, bf16[96,1024]{1,0:T(8,128)(2,1)} %up_in.1), custom_call_target="tpu_custom_call" | custom-call | flops 14495514624 | bytes 8388608 | tf_op jit(solution)/shard_map/pallas_call | solution.py:614
  140.1 0.7 copy.12
  140.8 0.6 copy.15
  141.4 1.1 copy.13
  142.5 1.1 copy.14

commit v3 on v2

--- a/solution.py
+++ b/solution.py
@@ -307,7 +307,6 @@
     for delta in range(1, 8):
         send(TC, TR.at[d], tr_s.at[delta], tr_r.at[d], dnb(delta))
     TR[d] = TC[...]
-    each(0, 4, lambda i: gathered(0, i))
 
     def own_chunk(g, delta, piece):
         return EP[g, piece, lanes(((z + delta + 8) % 8) // 2, 2 * ROWS)]
@@ -329,13 +328,29 @@
         ES[way, steps, piece] = value.astype(BF16)
         chunk_copy(way, steps, piece).start()
 
-    def token_grads(g, start, stop):
+    def shard_product(g, i, side):
+        j = shard_at(i)
+        rows = G[g, :, :, :, lanes(j, SH)].reshape(TOK, SH)
+        return fma_dot(rows, W[j, :, :, lanes(side, HALF)].reshape(SH, HALF), ((1,), (0,)))
+
+    def add_shard(g, i):
+        gathered(g, i)
+        for side in range(2):
+            both = shard_product(g, i, side)
+            for half in range(2):
+                term = both[:, half * QUARTER : (half + 1) * QUARTER]
+                if isinstance(i, int):
+                    EP[g, 2 * side + half] = term
+                else:
+                    EP[g, 2 * side + half] += term
+
+    def add_last_shard(g):
+        gathered(g, 3)
+
         def step(side):
-            both = fma_dot(
-                G[g].reshape(TOK, 4 * SH), W[:, :, :, lanes(side, HALF)].reshape(4 * SH, HALF), ((1,), (0,))
-            )
-            EP[g, 2 * side] = both[:, :QUARTER]
-            EP[g, 2 * side + 1] = both[:, QUARTER:]
+            both = shard_product(g, 3, side)
+            EP[g, 2 * side] += both[:, :QUARTER]
+            EP[g, 2 * side + 1] += both[:, QUARTER:]
 
             @pl.when((zl == g) & (side == 0))
             def _():
@@ -357,7 +372,7 @@
                 send_chunk(g, 0, 3, 2, False)
                 send_chunk(g, 0, 3, 3, False)
 
-        each(start, stop, step)
+        each(0, 2, step)
 
     def ring_step(g, owner, steps, start, stop):
         @pl.when((zl == g) == owner)
@@ -426,16 +441,19 @@
         return DR[way, kind].astype(F32)
 
     cut = SH // 2
-    token_grads(0, 0, 2)
-    each(0, 4, lambda i: relay_piece(1, i))
+    add_shard(0, 0)
+    each(1, 3, lambda i: add_shard(0, i))
+    each(0, 2, lambda i: relay_piece(1, i))
+    add_last_shard(0)
+    each(2, 4, lambda i: relay_piece(1, i))
     ring_step(0, False, 3, 2, 4)
     ring_step(0, True, 2, 0, 2)
     each(0, 4, lambda i: sibling_piece(1, i))
-    each(0, 4, lambda i: gathered(1, i))
-    token_grads(1, 0, 1)
+    add_shard(1, 0)
     ring_step(0, True, 2, 2, 4)
-    token_grads(1, 1, 2)
+    each(1, 3, lambda i: add_shard(1, i))
     ring_step(0, False, 1, 0, 2)
+    add_last_shard(1)
     ring_step(1, False, 3, 2, 4)
     ring_step(0, False, 1, 2, 4)
     part = shard_grad(2)
@@ -443,13 +461,13 @@
     send_grad(1, 0, part[cut:])
     ring_step(1, True, 2, 0, 2)
     ring_step(1, True, 2, 2, 4)
-    part = shard_grad(1)
-    send_grad(0, 1, part[cut:])
-    PW[0] = part[:cut]
     ring_step(1, False, 1, 0, 2)
     ring_step(1, False, 1, 2, 4)
     finish(0, 0, 4)
     finish(1, 0, 4)
+    part = shard_grad(1)
+    send_grad(0, 1, part[cut:])
+    PW[0] = part[:cut]
     part = shard_grad(-1)
     send_grad(1, 1, part[:cut])
     PW[1] = part[cut:]

time: 145 us -> 143 us (0.986)
  no operation moved by 1% of the time
where the time goes in v3:
time: 143 us
  Pallas kernels  139 us (97%)
  local copies, waits for them, and re-layouts  3.56 us (2%)
    pallas_call x1, Pallas kernels, on_device(): pl.pallas_call(kernel, out_shape=tuple((pltpu.VMEM(shape.shape, shape.dty...  139 us
    unnamed x4, local copies, waits for them, and re-layouts  3.56 us

profile of v3, /device:TPU:1, one launch (start us, length us, event | category | flops | bytes accessed | tf_op | source)
XLA Modules:
  0.0 143.0 jit_solution(10744486916678940299)
XLA Ops:
  0.6 138.8 %shard_map.75 = (bf16[96,1024]{1,0:T(8,128)(2,1)S(1)}, bf16[768,1024]{1,0:T(8,128)(2,1)S(1)}, f32[384,1024]{1,0:T(8,128)S(1)}, f32[7,64]{1,0:T(8,128)S(1)}) custom-call(bf16[768,1024]{1,0:T(8,128)(2,1)} %tok_in.1, bf16[2,192,1024]{2,1,0:T(8,128)(2,1)} %bitcast.7, f32[7,64]{1,0:T(8,128)} %taps_ref.1, bf16[96,1024]{1,0:T(8,128)(2,1)} %up_in.1), custom_call_target="tpu_custom_call" | custom-call | flops 14495514624 | bytes 8388608 | tf_op jit(solution)/shard_map/pallas_call | solution.py:632
  139.4 0.7 copy.12
  140.1 0.6 copy.15
  140.7 1.1 copy.13
  141.9 1.1 copy.14

commit v4 on v3

--- a/solution.py
+++ b/solution.py
@@ -198,12 +198,13 @@
         def _():
             chip_sum(u - 1)
 
-        @pl.when(u >= 4)
-        def _():
-            relay(u - 3)
+        @pl.when(u >= 5)
+        def _():
+            relay(u - 4)
 
     each(0, 8, project_step)
     chip_sum(7)
+    relay(4)
     relay(5)
 
     def mixed_rows(j):
@@ -276,8 +277,9 @@
         G[g, x, k, :, lanes(3 * j + 2, CH)] = (grad_mixed * QKV[g, j, :, CH : 2 * CH]).astype(BF16)
         TS[g, j] = jnp.concatenate(tap_sums + [jnp.zeros((1, CH), F32)], axis=0)
 
-        own_piece(g, j, 0).start()
-        own_piece(g, j, 1).start()
+        if g == 0:
+            own_piece(g, j, 0).start()
+            own_piece(g, j, 1).start()
 
     def relay_piece(g, i):
         j, to_left = shard_at(i), i % 2
@@ -296,6 +298,8 @@
     def second_group(i):
         filter_step(1, i)
         sibling_piece(0, i)
+        own_piece(1, shard_at(i), 0).start()
+        own_piece(1, shard_at(i), 1).start()
 
     each(0, 4, lambda i: filter_step(0, i))
     each(0, 4, lambda i: relay_piece(0, i))

time: 143 us -> 143 us (level)
  no operation moved by 1% of the time
where the time goes in v4:
time: 143 us
  Pallas kernels  139 us (97%)
  local copies, waits for them, and re-layouts  3.56 us (2%)
    pallas_call x1, Pallas kernels, on_device(): pl.pallas_call(kernel, out_shape=tuple((pltpu.VMEM(shape.shape, shape.dty...  139 us
    unnamed x4, local copies, waits for them, and re-layouts  3.56 us

profile of v4, /device:TPU:1, one launch (start us, length us, event | category | flops | bytes accessed | tf_op | source)
XLA Modules:
  0.0 143.2 jit_solution(1929763707273363676)
XLA Ops:
  0.6 139.0 %shard_map.75 = (bf16[96,1024]{1,0:T(8,128)(2,1)S(1)}, bf16[768,1024]{1,0:T(8,128)(2,1)S(1)}, f32[384,1024]{1,0:T(8,128)S(1)}, f32[7,64]{1,0:T(8,128)S(1)}) custom-call(bf16[768,1024]{1,0:T(8,128)(2,1)} %tok_in.1, bf16[2,192,1024]{2,1,0:T(8,128)(2,1)} %bitcast.7, f32[7,64]{1,0:T(8,128)} %taps_ref.1, bf16[96,1024]{1,0:T(8,128)(2,1)} %up_in.1), custom_call_target="tpu_custom_call" | custom-call | flops 14495514624 | bytes 8388608 | tf_op jit(solution)/shard_map/pallas_call | solution.py:636
  139.6 0.7 copy.12
  140.3 0.6 copy.15
  140.9 1.1 copy.13
  142.0 1.1 copy.14
